TPU v7x, 32 devices: a whole 2x2x4 slice. The times are simulated.
32 devices in a mesh: cfg: 1, node: 32 (over z, y, x, core), pair: 1.
Axes of the slice: x: 2, y: 2, z: 4, core: 2. Of those that a mesh axis runs over, the one named last changes fastest.
Arguments:
- node_blocks: float32 [256, 2, 256, 256], P(('cfg', 'node'), None, None, 'pair'), may hold values from -1.5 to 1.5
- node_slot: int32 [256], replicated, may hold values from 0 to 255, as said below
- pair_list: int32 [128, 2], replicated, may hold values from 0 to 255, as said below
- second_list: int32 [128, 2], replicated, may hold values from 0 to 127, as said below
- targets: int32 [128], replicated, may hold values from 0 to 63, as said below
- spin_signs: int32 [128], replicated, may hold values from -1 to 1, as said below
Outputs:
- results: float32 [64, 2, 256, 256], P(('cfg', 'node'), None, None, 'pair')
Inputs may be any that keep to these rules, and one draw needn't show every extreme that they name: `node_slot`: A permutation of the slots. `pair_list`: rows b * 4 to (b + 1) * 4 - 1 form block b. The first node of a pair in block b sits at a slot of b * 8 to (b + 1) * 8 - 1. For every block b and every owner o, at most 1 pair of block b has its second node at slots o * 8 to (o + 1) * 8 - 1; one owner supplies exactly 1 such node to every block. `second_list`: rows b * 4 to (b + 1) * 4 - 1 form block b. The first pair of a product in block b lies in block b of the pairs. For every block b and owner o, at most 1 product of block b has its second pair in block o of the pairs; one owner supplies exactly 1 such pair product to every block. `targets`: products of block b target results b * 2 to (b + 1) * 2 - 1. `spin_signs`: each entry is -1 or 1.
All inputs are finite; a program needn't handle non-finite values.
Results may differ from a plain program's by a relative error of at most 0.000098.
Values sent between devices are 32-bit elements; how exact they have to be, the bound alone decides.
A program may use at most 128 MiB of HBM per device.

v0:
```python
import functools
import math

import jax
import jax.numpy as jnp
from jax import lax
from jax.experimental import pallas as pl
from jax.experimental.pallas import tpu as pltpu
from jax.sharding import PartitionSpec as P

GROUP = 8
STEPS = (8, 9, 11)
EXTRA = 3
CHUNKS = 4
MESH = pl.DeviceIdType.MESH
RES_COL = 2


def complex_product(left_side, right_side):
    half_width = right_side.shape[3]
    stacked_left = jnp.concatenate([left_side[:, 0], left_side[:, 1]], axis=2)
    real_right = jnp.concatenate([right_side[:, 0], -right_side[:, 1]], axis=1)
    imag_right = jnp.concatenate([right_side[:, 1], right_side[:, 0]], axis=1)
    stacked_right = jnp.concatenate([real_right, imag_right], axis=2)
    joined = jnp.einsum(
        "jmk,jkn->jmn",
        stacked_left,
        stacked_right,
        precision=lax.Precision.HIGH,
        preferred_element_type=jnp.float32,
    )
    return jnp.stack([joined[:, :, :half_width], joined[:, :, half_width:]], axis=1)


def exchange_kernel(
    lanes, planes, count, picks, capacity, share, chunks,
    send_table, hot_table, kind_table, place_table, items, out, *scratch,
):
    pieces, came, hot = scratch[:chunks], scratch[chunks : 2 * chunks], scratch[2 * chunks : 3 * chunks]
    packed, outgoing, s1, r1, s2, r2, s3, r3, s4, r4, own1, own4 = scratch[3 * chunks :]
    column = lax.axis_index("node")
    plane, lane = column // lanes, column % lanes
    rows = items.shape[2]
    part = rows // lanes
    step = part // chunks
    size = capacity + share

    def beside(e):
        return {"node": plane * lanes + lax.rem(lane + e, lanes)}

    def facing(d):
        low = (plane % 2) * 2
        high = ((plane // 2) % 2) * 4
        return plane + (1 - low if d % 2 else 0) + (2 - high if d >= 2 else 0)

    def along(d):
        return {"node": facing(d) * lanes + lane}

    def size_of(d):
        return size + (EXTRA if d == 1 else 0)

    def offset_of(d):
        return (d - 1) * size + (EXTRA if d > 1 else 0)

    barrier = pltpu.get_barrier_semaphore()
    for e in range(1, lanes):
        pl.semaphore_signal(barrier, inc=1, device_id=beside(e), device_id_type=MESH)
    for d in range(1, planes):
        pl.semaphore_signal(barrier, inc=1, device_id=along(d), device_id_type=MESH)
    pl.semaphore_wait(barrier, lanes - 1 + planes - 1)

    def rows_of(owner, c):
        return pl.ds(pl.multiple_of(owner * part + c * step, step), step)

    first, second, third, last = {}, {}, {}, {}

    def spread(c):
        group = []
        for e in range(1, lanes):
            copy = pltpu.make_async_remote_copy(
                src_ref=items.at[:, :, rows_of(lax.rem(lane + e, lanes), c), :],
                dst_ref=pieces[c].at[pl.ds(lane * count, count)],
                send_sem=s1.at[c, e - 1], recv_sem=r1.at[c, e - 1],
                device_id=beside(e), device_id_type=MESH,
            )
            copy.start()
            group.append(copy)
        copy = pltpu.make_async_copy(
            items.at[:, :, rows_of(lane, c), :], pieces[c].at[pl.ds(lane * count, count)], own1.at[c]
        )
        copy.start()
        first[c] = (group, copy)

    def gathered(c):
        for copy in first[c][0]:
            copy.wait_recv()
        first[c][1].wait()

    def pack(c):
        for d in range(1, planes):
            target = facing(d)

            def move(k, carry, d=d, target=target):
                packed[c, d - 1, k] = pieces[c][send_table[target, k]]
                return carry

            lax.fori_loop(0, size_of(d), move, 0)

    def cross(c):
        second[c] = []
        for d in range(1, planes):
            copy = pltpu.make_async_remote_copy(
                src_ref=packed.at[c, d - 1, pl.ds(0, size_of(d))],
                dst_ref=came[c].at[pl.ds(offset_of(d), size_of(d))],
                send_sem=s2.at[c, d - 1], recv_sem=r2.at[c, d - 1],
                device_id=along(d), device_id_type=MESH,
            )
            copy.start()
            second[c].append(copy)

    def crossed(c):
        for copy in second[c]:
            copy.wait_recv()

    def pass_on(c):
        for i in range(share):
            here = pieces[c][hot_table[0, i]]
            there = came[c][hot_table[1, i]]
            hot[c][plane * share + i] = jnp.where(hot_table[2, i] == 1, here, there)
        third[c] = []
        for d in range(1, planes):
            copy = pltpu.make_async_remote_copy(
                src_ref=hot[c].at[pl.ds(plane * share, share)],
                dst_ref=hot[c].at[pl.ds(plane * share, share)],
                send_sem=s3.at[c, d - 1], recv_sem=r3.at[c, d - 1],
                device_id=along(d), device_id_type=MESH,
            )
            copy.start()
            third[c].append(copy)

    def deliver(c):
        for copy in third[c]:
            copy.wait_recv()
        sent = []
        for e in range(lanes):
            target = lax.rem(lane + e, lanes)

            def move(j, carry, e=e, target=target):
                kind, place = kind_table[target, j], place_table[target, j]
                a = pieces[c][jnp.where(kind == 0, place, 0)]
                b = came[c][jnp.where(kind == 1, place, 0)]
                h = hot[c][jnp.where(kind == 2, place, 0)]
                outgoing[c, e, j] = jnp.where(kind == 0, a, jnp.where(kind == 1, b, h))
                return carry

            lax.fori_loop(0, picks, move, 0)
            if e == 0:
                own = pltpu.make_async_copy(outgoing.at[c, e], out.at[:, :, rows_of(lane, c), :], own4.at[c])
                own.start()
                continue
            copy = pltpu.make_async_remote_copy(
                src_ref=outgoing.at[c, e],
                dst_ref=out.at[:, :, rows_of(lane, c), :],
                send_sem=s4.at[c, e - 1], recv_sem=r4.at[c, e - 1],
                device_id=beside(e), device_id_type=MESH,
            )
            copy.start()
            sent.append(copy)
        last[c] = (sent, own)

    spread(0)
    for c in range(chunks):
        gathered(c)
        if c + 1 < chunks:
            spread(c + 1)
        pack(c)
        if c < 2:
            cross(c)
    for c in range(chunks):
        crossed(c)
        if c + 2 < chunks:
            cross(c + 2)
        pass_on(c)
        if c > 0:
            deliver(c - 1)
    deliver(chunks - 1)

    for c in range(chunks):
        for copy in first[c][0] + second[c] + third[c]:
            copy.wait_send()
        for copy in last[c][0]:
            copy.wait()
        last[c][1].wait()


def exchange(lanes, planes, picks, capacity, share, collective_id, tables, items):
    count, _, rows, width = items.shape
    part = rows // lanes
    chunks = CHUNKS if part % (8 * CHUNKS) == 0 else 1
    step = part // chunks
    size = capacity + share
    block = (2, step, width)
    smem = pl.BlockSpec(memory_space=pltpu.SMEM)
    sems = [(chunks, n) for n in (lanes - 1, lanes - 1, planes - 1, planes - 1, planes - 1, planes - 1, lanes - 1, lanes - 1)]
    return pl.pallas_call(
        functools.partial(exchange_kernel, lanes, planes, count, picks, capacity, share, chunks),
        out_shape=jax.ShapeDtypeStruct((picks, 2, rows, width), jnp.float32),
        in_specs=[smem] * 4 + [pl.BlockSpec(memory_space=pl.ANY)],
        out_specs=pl.BlockSpec(memory_space=pl.ANY),
        scratch_shapes=[pltpu.VMEM((lanes * count, *block), jnp.float32)] * chunks
        + [pltpu.VMEM(((planes - 1) * size + EXTRA, *block), jnp.float32)] * chunks
        + [pltpu.VMEM((planes * share, *block), jnp.float32)] * chunks
        + [pltpu.VMEM((chunks, planes - 1, size + EXTRA, *block), jnp.float32)]
        + [pltpu.VMEM((chunks, lanes, picks, *block), jnp.float32)]
        + [pltpu.SemaphoreType.DMA(s) for s in sems]
        + [pltpu.SemaphoreType.DMA((chunks,))] * 2,
        compiler_params=pltpu.CompilerParams(
            collective_id=collective_id, has_side_effects=True, vmem_limit_bytes=40 * 2**20
        ),
    )(*tables, items)


def fetch(items, wanted, columns, column, first_id):
    count, _, rows, width = items.shape
    picks = wanted.shape[1]
    lanes = math.gcd(GROUP, columns)
    planes = columns // lanes
    plane, lane = column // lanes, column % lanes
    part = rows // lanes
    in_plane = [[p * lanes + q for q in range(lanes)] for p in range(planes)]
    in_line = [[p * lanes + q for p in range(planes)] for q in range(lanes)]
    held = lanes * count
    share = -(-count // planes)

    owners = wanted // count
    supplied = jnp.sum((owners.reshape(-1)[:, None] == jnp.arange(columns)[None, :]).astype(jnp.int32), axis=0)
    common = jnp.argmax(supplied).astype(jnp.int32)
    common_plane, common_lane = common // lanes, common % lanes
    is_common = owners == common

    flat = jnp.where(is_common, -1, wanted).reshape(planes, lanes * picks)
    need = jnp.any(flat[:, :, None] == jnp.arange(planes * held)[None, None, :], axis=1)
    need = need.reshape(planes, planes, held).transpose(1, 2, 0)
    foreign = jnp.arange(planes)[:, None] != jnp.arange(planes)[None, :]
    need = need & foreign[:, None, :]
    counted = need.astype(jnp.int32)
    lower = (jnp.arange(held)[:, None] > jnp.arange(held)[None, :]).astype(jnp.int32)
    rank = jnp.sum(lower[None, :, :, None] * counted[:, None, :, :], axis=2)
    totals = jnp.sum(counted, axis=1)
    near = (jnp.arange(planes)[:, None] // 2) == (jnp.arange(planes)[None, :] // 2)
    most = jnp.max(totals - EXTRA * near.astype(jnp.int32))

    mine = lax.dynamic_index_in_dim(counted, plane, 0, keepdims=False)
    my_rank = lax.dynamic_index_in_dim(rank, plane, 0, keepdims=False)
    to_me = lax.dynamic_index_in_dim(rank, plane, 2, keepdims=False)
    asked = lax.dynamic_slice_in_dim(wanted, plane * lanes, lanes, 0)
    asked_plane, asked_item = asked // held, asked % held
    asked_common = (asked // count) == common
    asked_rank = to_me[asked_plane, asked_item]
    shares = jnp.minimum(jnp.arange(planes * share), count - 1).reshape(planes, share)

    def listing(capacity, first=False):
        chosen = mine[:, :, None] * (my_rank[:, :, None] == jnp.arange(capacity)).astype(jnp.int32)
        listed = jnp.sum(chosen * jnp.arange(held)[:, None, None], axis=0)
        parts = [common_lane * count + shares, listed]
        return jnp.concatenate(parts if first else parts[::-1], axis=1)

    def general(capacity):
        def run(items):
            cut = items.reshape(count, 2, lanes, part, width).transpose(2, 0, 1, 3, 4)
            pieces = lax.all_to_all(cut, "node", 0, 0, axis_index_groups=in_plane, tiled=True)
            pieces = pieces.reshape(held, 2, part, width)
            listed = listing(capacity)
            size = capacity + share
            packed = jnp.take(pieces, listed.reshape(-1), axis=0).reshape(planes, size, 2, part, width)
            came = lax.all_to_all(packed, "node", 0, 0, axis_index_groups=in_line, tiled=True)
            own_share = lax.dynamic_index_in_dim(came, common_plane, 0, keepdims=False)[capacity:]
            all_common = lax.all_gather(own_share, "node", axis=0, axis_index_groups=in_line, tiled=True)
            store = jnp.concatenate([pieces, came.reshape(planes * size, 2, part, width), all_common], axis=0)
            at = jnp.where(asked_plane == plane, asked_item, held + asked_plane * size + asked_rank)
            at = jnp.where(asked_common, held + planes * size + asked % count, at)
            outgoing = jnp.take(store, at.reshape(-1), axis=0).reshape(lanes, picks, 2, part, width)
            arrived = lax.all_to_all(outgoing, "node", 0, 0, axis_index_groups=in_plane, tiled=True)
            return arrived.transpose(1, 2, 0, 3, 4).reshape(picks, 2, rows, width)

        return run

    def direct(capacity, collective_id):
        size = capacity + share
        distance = plane ^ asked_plane

        def offset(d):
            return jnp.maximum((d - 1) * size + EXTRA * (d > 1), 0)

        kind = jnp.where(asked_common, 2, jnp.where(distance == 0, 0, 1)).astype(jnp.int32)
        place = jnp.where(distance == 0, asked_item, offset(distance) + share + asked_rank)
        place = jnp.where(asked_common, asked % count, place).astype(jnp.int32)
        away = plane ^ common_plane
        here = common_lane * count + lax.dynamic_index_in_dim(shares, plane, 0, keepdims=False)
        there = offset(away) + jnp.arange(share)
        local = jnp.broadcast_to((away == 0).astype(jnp.int32), (share,))
        hot_table = jnp.stack([here, there, local]).astype(jnp.int32)

        def run(items):
            tables = (listing(capacity + EXTRA, True).astype(jnp.int32), hot_table, kind, place)
            return exchange(lanes, planes, picks, capacity, share, collective_id, tables, items)

        return run

    limit = min(held, lanes * picks)
    steps = [c for c in STEPS if c + EXTRA < limit and planes == 4]
    if not steps:
        return general(limit)(items)
    branch = jnp.sum((most > jnp.array(steps, jnp.int32)).astype(jnp.int32))
    branches = [direct(c, first_id + i) for i, c in enumerate(steps)] + [general(limit)]
    return lax.switch(branch, branches, items)


def per_device(node_blocks, node_slot, pair_list, second_list, targets, spin_signs):
    columns = lax.axis_size("node")
    column = lax.axis_index("node")
    node_col = node_blocks.shape[0]
    pair_col = pair_list.shape[0] // columns
    block_start = column * pair_col
    own_pairs = lax.dynamic_slice_in_dim(pair_list, block_start, pair_col, 0)
    first_slot = node_slot[own_pairs[:, 0]] - column * node_col
    whole_nodes = lax.all_gather(node_blocks, "pair", axis=3, tiled=True)
    first_nodes = jnp.take(whole_nodes, first_slot, axis=0)
    wanted = node_slot[pair_list[:, 1]].reshape(columns, pair_col)
    second_nodes = fetch(node_blocks, wanted, columns, column, 0)
    products = complex_product(first_nodes, second_nodes)
    whole_products = lax.all_gather(products, "pair", axis=3, tiled=True)
    own_seconds = lax.dynamic_slice_in_dim(second_list, block_start, pair_col, 0)
    left_side = jnp.take(whole_products, own_seconds[:, 0] - block_start, axis=0)
    right_side = fetch(products, second_list[:, 1].reshape(columns, pair_col), columns, column, len(STEPS))
    own_signs = lax.dynamic_slice_in_dim(spin_signs, block_start, pair_col, 0).astype(jnp.float32)
    seconds = complex_product(left_side, right_side) * own_signs[:, None, None, None]
    return seconds, column


def solution(mesh):
    placed = (P(("cfg", "node"), None, None, "pair"), P(), P(), P(), P(), P())

    def run(node_blocks, node_slot, pair_list, second_list, targets, spin_signs):
        res_col = RES_COL

        def body(*args):
            seconds, column = per_device(*args)
            pair_col = seconds.shape[0]
            own = lax.dynamic_slice_in_dim(args[4], column * pair_col, pair_col, 0) - column * res_col
            return jnp.stack(
                [
                    jnp.sum(jnp.where((own == r)[:, None, None, None], seconds, 0.0), axis=0)
                    for r in range(res_col)
                ]
            )

        return jax.shard_map(
            body, mesh=mesh, in_specs=placed, out_specs=P(("cfg", "node"), None, None, "pair"), check_vma=False
        )(node_blocks, node_slot, pair_list, second_list, targets, spin_signs)

    return run
```

profile of v0, /device:TPU:0, one launch (start us, length us, event | category | flops | bytes accessed | tf_op | source)
XLA Modules:
  0.0 261.4 jit_solution(12145021146860012719)
XLA Ops:
  0.0 0.7 fusion.74
  0.7 1.3 gather_fusion.6
  2.1 0.6 iota_reduce_fusion.1
  2.9 0.6 select_select_fusion.7
  3.4 0.7 slice_bitcast_fusion.8
  4.3 0.7 iota_reduce_fusion
  5.0 0.6 select_select_fusion.6
  5.9 1.1 fusion.64
  7.3 0.4 multiply_reduce_fusion.8
  7.7 0.8 gather_fusion.7
  11.6 0.7 fusion.52
  12.3 1.9 fusion.69
  14.9 121.4 %conditional.2 = (f32[4,2,256,256]{3,2,1,0:T(8,128)}, f32[4,1,256,256]{3,2,1,0:T(8,128)}, f32[4,1,256,256]{3,2,1,0:T(8,128)S(1)}, f32[4,1,256,256]{3,2,1,0:T(8,1...) conditional(s32[]{:T(128)} %clamp.6, (s32[]{:T(128)}, ...), branch_computations={%region_7.9_spmd, %region_9.11_spmd, %region_11.13_spmd, %region_1... | conditional | flops 9605181 | bytes 155599680 | solution.py:316
  15.0 0.3 multiply_reduce_fusion.1
  15.4 115.0 %branch_1_fun.2 = f32[4,2,256,256]{3,2,1,0:T(8,128)S(1)} custom-call(s32[4,14]{1,0:T(4,128)S(1)} %pad_add_fusion.1.send_table, s32[3,2]{1,0:T(4,128)S(1)} %get-tuple-element.363.hot_table, s32[8,4]{1,0:T(8,128)S(1)} %get-tuple-element.364.kind_table, s32[8,4]{1,0:T(8,128)S(1)} %select_select_fusion.1.place_table, f32[8,2,256,256]{3,2,1,0:T(8,128)} %get-tuple-element.374.items), custom_call_target="tpu_custom_call" | custom-call | tf_op jit(solution)/shard_map/cond/branch_1_fun/pallas_call | solution.py:205
  130.5 1.2 fusion.83
  131.7 0.4 copy-done.16
  132.1 1.6 copy.284
  134.0 2.3 copy.319
  136.3 1.1 neg.36
  137.5 0.6 gather_fusion.4
  138.2 2.9 %gather_fusion.5 = f32[4,2,256,256]{3,2,1,0:T(8,128)S(1)} fusion(f32[8,2,256,256]{3,2,1,0:T(8,128)} %param.16, s32[1024]{0:T(1024)S(1)} %pad_clamp_fusion.6), kind=kCustom, calls=%fused_computation.5 | custom fusion | bytes 4194320 | tf_op jit(solution)/shard_map/jit(_take)/gather | solution.py:328
  141.1 0.2 copy_select_fusion.1
  141.5 1.1 copy-done.19
  142.6 3.9 %fusion.8 = f32[4,256,512]{2,1,0:T(8,128)S(1)} fusion(f32[4,256,256]{2,1,0:T(8,128)} %get-tuple-element.942, f32[4,256,256]{2,1,0:T(8,128)S(1)} %get-tuple-element.941, f32[4,256,256]{2,1,0:T(8,128)S(1)} %copy-done.19, f32[4,256,256]{2,1,0:T(8,128)S(1)} %get-tuple-element.1000, f32[4,256,256]{2,1,0:T(8,128)S(1)} %get-tuple-element.999), kind=kOutput, calls=%fused_computation.86 | convolution fusion | flops 1614282752 | bytes 7340032 | tf_op jit(solution)/shard_map/jmk,jkn->jmn/dot_general | solution.py:25
  146.7 1.5 pad_maximum_fusion.2
  148.3 0.4 multiply_reduce_fusion.9
  148.7 0.8 gather_fusion.9
  151.9 0.6 squeeze.118
  153.8 94.4 %conditional.3 = (f32[4,2,256,256]{3,2,1,0:T(8,128)}, f32[4,1,256,256]{3,2,1,0:T(8,128)}, f32[4,1,256,256]{3,2,1,0:T(8,128)S(1)}, f32[4,1,256,256]{3,2,1,0:T(8,1...) conditional(s32[]{:T(128)} %clamp.7, (s32[]{:T(128)}, ...), branch_computations={%region_22.24_spmd, %region_24.26_spmd, %region_26.28_spmd, %regio... | conditional | flops 8212497 | bytes 137576128 | solution.py:316
  153.8 1.8 copy.204.items
  155.6 0.3 multiply_reduce_fusion.3
  156.2 87.1 %branch_0_fun.3 = f32[4,2,256,256]{3,2,1,0:T(8,128)S(1)} custom-call(s32[4,12]{1,0:T(4,128)S(1)} %pad_add_fusion.3.send_table, s32[3,1]{1,0:T(4,128)S(1)} %copy.203.hot_table, s32[8,4]{1,0:T(8,128)S(1)} %get-tuple-element.408.kind_table, s32[8,4]{1,0:T(8,128)S(1)} %select_select_fusion.3.place_table, f32[4,2,256,256]{3,2,1,0:T(8,128)S(1)} %copy.204.items), custom_call_target="tpu_custom_call" | custom-call | tf_op jit(solution)/shard_map/cond/branch_0_fun/pallas_call | solution.py:205
  243.4 1.2 fusion.85
  244.6 0.4 copy-done.11
  245.1 1.6 copy.296
  246.9 1.2 copy.331
  248.2 1.1 neg.37
  249.5 1.0 copy-done.10
  250.6 0.5 copy-done.23
  251.3 2.0 gather_fusion.8
  253.3 1.8 copy_select_fusion
  255.3 1.1 copy-done.20
  256.4 0.3 copy-done.22
  256.7 2.5 fusion.16
  259.4 0.5 copy-done.27
  259.9 0.4 select_reduce_fusion.1
  260.4 1.0 pad_maximum_fusion.3
  (100 shorter events, 4.7 us)
Async XLA Ops:
  0.0 0.7 copy-start
  7.7 4.6 %copy-start.25 = (s32[3]{0:T(128)S(1)}, s32[3]{0:T(128)}, u32[]{:S(2)}) copy-start(s32[3]{0:T(128)} %constant.445.clone) | copy-start | bytes 40
  130.5 1.7 copy-start.16
  132.1 1.8 copy-start.3
  136.3 1.1 copy-start.24
  136.3 1.8 copy-start.26
  141.3 1.2 copy-start.19
  243.4 1.7 copy-start.11
  245.1 1.8 copy-start.6
  248.2 1.3 copy-start.21
  248.2 2.3 copy-start.10
  250.5 0.7 copy-start.23
  255.1 1.2 copy-start.20
  255.2 1.5 copy-start.22
  259.2 0.7 copy-start.27
  259.8 1.6 copy-start.1
where the time goes:
time: 261 us
  Pallas kernels  202 us (77%)
  local copies, waits for them, and re-layouts  28.2 us (11%)
  other arithmetic  17.8 us (7%)
  between operations  6.68 us (3%)
  matrix products  6.42 us (2%)
    pallas_call x2, Pallas kernels, exchange(): pl.pallas_call(functools.partial(exchange_kernel, lanes, planes, count, p...  202 us
    cond x18, local copies, waits for them, and re-layouts  8.03 us
    dot_general x2, matrix products, complex_product(): jnp.einsum('jmk,jkn->jmn', stacked_left, stacked_right, precision=lax.Pre...  6.42 us

commit v1 on v0

--- a/solution.py
+++ b/solution.py
@@ -9,7 +9,7 @@
 from jax.sharding import PartitionSpec as P
 
 GROUP = 8
-STEPS = (8, 9, 11)
+STEPS = (8, 10)
 EXTRA = 3
 CHUNKS = 4
 MESH = pl.DeviceIdType.MESH
@@ -174,12 +174,9 @@
         if c + 1 < chunks:
             spread(c + 1)
         pack(c)
-        if c < 2:
-            cross(c)
+        cross(c)
     for c in range(chunks):
         crossed(c)
-        if c + 2 < chunks:
-            cross(c + 2)
         pass_on(c)
         if c > 0:
             deliver(c - 1)

time: 261 us -> 263 us (level); the launches traced: 261 us -> 268 us
  Pallas kernels: 202 us -> 209 us
    pallas_call x2, Pallas kernels: 202 us -> 209 us  [exchange(): pl.pallas_call(functools.partial(exchange_kernel, lanes, planes, count, p...]
where the time goes in v1:
time: 263 us; the launch traced here: 268 us
  Pallas kernels  209 us (79%)
  local copies, waits for them, and re-layouts  28.3 us (11%)
  other arithmetic  17.7 us (7%)
  between operations  6.81 us (3%)
  matrix products  6.42 us (2%)
    pallas_call x2, Pallas kernels, exchange(): pl.pallas_call(functools.partial(exchange_kernel, lanes, planes, count, p...  209 us
    cond x18, local copies, waits for them, and re-layouts  8.03 us
    dot_general x2, matrix products, complex_product(): jnp.einsum('jmk,jkn->jmn', stacked_left, stacked_right, precision=lax.Pre...  6.42 us

profile of v1, /device:TPU:0, one launch (start us, length us, event | category | flops | bytes accessed | tf_op | source)
XLA Modules:
  0.0 268.2 jit_solution(26664122798173044)
XLA Ops:
  0.0 0.7 fusion.73
  0.7 1.3 gather_fusion.6
  2.1 0.6 iota_reduce_fusion.1
  2.9 0.6 select_select_fusion.5
  3.4 0.7 slice_bitcast_fusion.8
  4.3 0.7 iota_reduce_fusion
  5.0 0.6 select_select_fusion.4
  5.9 1.1 fusion.63
  7.3 0.4 multiply_reduce_fusion.6
  7.7 0.8 gather_fusion.7
  11.6 0.7 fusion.52
  12.3 1.9 fusion.68
  14.9 122.6 %conditional.2 = (f32[4,2,256,256]{3,2,1,0:T(8,128)}, f32[4,1,256,256]{3,2,1,0:T(8,128)}, f32[4,1,256,256]{3,2,1,0:T(8,128)S(1)}, f32[4,1,256,256]{3,2,1,0:T(8,1...) conditional(s32[]{:T(128)} %clamp.6, (s32[]{:T(128)}, ...), branch_computations={%region_7.9_spmd, %region_9.11_spmd, %region_11.13_spmd} | conditional | flops 9605181 | bytes 155599680 | solution.py:313
  15.0 0.3 multiply_reduce_fusion.1
  15.5 116.2 %branch_1_fun.2 = f32[4,2,256,256]{3,2,1,0:T(8,128)S(1)} custom-call(s32[4,15]{1,0:T(4,128)S(1)} %pad_add_fusion.1.send_table, s32[3,2]{1,0:T(4,128)S(1)} %get-tuple-element.281.hot_table, s32[8,4]{1,0:T(8,128)S(1)} %get-tuple-element.282.kind_table, s32[8,4]{1,0:T(8,128)S(1)} %select_select_fusion.1.place_table, f32[8,2,256,256]{3,2,1,0:T(8,128)} %get-tuple-element.292.items), custom_call_target="tpu_custom_call" | custom-call | tf_op jit(solution)/shard_map/cond/branch_1_fun/pallas_call | solution.py:202
  131.7 1.2 fusion.82
  132.9 0.4 copy-done.13
  133.4 1.6 copy.228
  135.2 2.3 copy.260
  137.5 1.1 neg.30
  138.7 0.6 gather_fusion.4
  139.4 2.9 %gather_fusion.5 = f32[4,2,256,256]{3,2,1,0:T(8,128)S(1)} fusion(f32[8,2,256,256]{3,2,1,0:T(8,128)} %param.14, s32[1024]{0:T(1024)S(1)} %pad_clamp_fusion.6), kind=kCustom, calls=%fused_computation.5 | custom fusion | bytes 4194320 | tf_op jit(solution)/shard_map/jit(_take)/gather | solution.py:325
  142.3 0.2 copy_select_fusion.1
  142.7 1.1 copy-done.15
  143.8 3.9 %fusion.8 = f32[4,256,512]{2,1,0:T(8,128)S(1)} fusion(f32[4,256,256]{2,1,0:T(8,128)} %get-tuple-element.700, f32[4,256,256]{2,1,0:T(8,128)S(1)} %get-tuple-element.699, f32[4,256,256]{2,1,0:T(8,128)S(1)} %copy-done.15, f32[4,256,256]{2,1,0:T(8,128)S(1)} %get-tuple-element.754, f32[4,256,256]{2,1,0:T(8,128)S(1)} %get-tuple-element.753), kind=kOutput, calls=%fused_computation.76 | convolution fusion | flops 1614282752 | bytes 7340032 | tf_op jit(solution)/shard_map/jmk,jkn->jmn/dot_general | solution.py:25
  147.9 1.5 pad_maximum_fusion.2
  149.6 0.4 multiply_reduce_fusion.7
  149.9 0.8 gather_fusion.9
  153.2 0.7 squeeze.106
  155.2 99.8 %conditional.3 = (f32[4,2,256,256]{3,2,1,0:T(8,128)}, f32[4,1,256,256]{3,2,1,0:T(8,128)}, f32[4,1,256,256]{3,2,1,0:T(8,128)S(1)}, f32[4,1,256,256]{3,2,1,0:T(8,1...) conditional(s32[]{:T(128)} %clamp.7, (s32[]{:T(128)}, ...), branch_computations={%region_20.22_spmd, %region_22.24_spmd, %region_24.26_spmd} | conditional | flops 8212497 | bytes 137576128 | solution.py:313
  155.2 1.8 copy.166.items
  157.0 0.3 multiply_reduce_fusion.2
  157.6 92.6 %branch_0_fun.3 = f32[4,2,256,256]{3,2,1,0:T(8,128)S(1)} custom-call(s32[4,12]{1,0:T(4,128)S(1)} %pad_add_fusion.2.send_table, s32[3,1]{1,0:T(4,128)S(1)} %copy.165.hot_table, s32[8,4]{1,0:T(8,128)S(1)} %get-tuple-element.310.kind_table, s32[8,4]{1,0:T(8,128)S(1)} %select_select_fusion.2.place_table, f32[4,2,256,256]{3,2,1,0:T(8,128)S(1)} %copy.166.items), custom_call_target="tpu_custom_call" | custom-call | tf_op jit(solution)/shard_map/cond/branch_0_fun/pallas_call | solution.py:202
  250.2 1.2 fusion.83
  251.5 0.4 copy-done.9
  251.9 1.6 copy.238
  253.8 1.2 copy.268
  255.0 1.1 neg.31
  256.3 1.0 copy-done.8
  257.5 0.5 copy-done.19
  258.1 2.0 gather_fusion.8
  260.1 1.8 copy_select_fusion
  262.1 1.1 copy-done.16
  263.2 0.3 copy-done.18
  263.5 2.5 fusion.16
  266.2 0.5 copy-done.23
  266.8 0.4 select_reduce_fusion.1
  267.2 1.0 pad_maximum_fusion.3
  (99 shorter events, 4.6 us)
Async XLA Ops:
  0.0 0.7 copy-start
  7.7 4.6 %copy-start.21 = (s32[2]{0:T(128)S(1)}, s32[2]{0:T(128)}, u32[]{:S(2)}) copy-start(s32[2]{0:T(128)} %constant.420.clone) | copy-start | bytes 28
  131.7 1.7 copy-start.13
  133.4 1.8 copy-start.3
  137.5 1.1 copy-start.20
  137.5 1.8 copy-start.22
  142.6 1.2 copy-start.15
  250.2 1.7 copy-start.9
  251.9 1.8 copy-start.5
  255.0 1.3 copy-start.17
  255.0 2.3 copy-start.8
  257.3 0.7 copy-start.19
  262.0 1.2 copy-start.16
  262.0 1.5 copy-start.18
  266.0 0.7 copy-start.23
  266.7 1.6 copy-start.1
